TPU v7x, 32 devices: a whole 2x2x4 slice. The times are simulated.
32 devices in a mesh: shard: 2 (over x), ctx: 4 (over z), tp: 4 (over y, core).
Axes of the slice: x: 2, y: 2, z: 4, core: 2. Of those that a mesh axis runs over, the one named last changes fastest.
Arguments:
- tokens: bfloat16 [2, 2560, 1024], P('shard', 'ctx'), may hold values from -6 to 6
- block_tokens: int32 [2, 4], P('shard'), may hold values from 1 to 640, 2048 in all within a row
- ln1_gain: bfloat16 [2, 1024], replicated, may hold values from 0.099609375 to 1.8984375
- ln1_bias: bfloat16 [2, 1024], replicated, may hold values from -1.5 to 1.5
- w_qkv: bfloat16 [2, 1024, 3072], P(None, ('shard', 'ctx'), 'tp'), may hold values from -0.1875 to 0.1875
- b_qv: bfloat16 [2, 2048], P(None, 'tp'), may hold values from -1.5 to 1.5
- w_out: bfloat16 [2, 1024, 1024], P(None, ('shard', 'ctx'), 'tp'), may hold values from -6 to 6
- b_out: bfloat16 [2, 1024], replicated, may hold values from -1.5 to 1.5
- ln2_gain: bfloat16 [2, 1024], replicated, may hold values from 0.099609375 to 1.8984375
- ln2_bias: bfloat16 [2, 1024], replicated, may hold values from -1.5 to 1.5
- w_up: bfloat16 [2, 1024, 4096], P(None, ('shard', 'ctx'), 'tp'), may hold values from -0.1875 to 0.1875
- b_up: bfloat16 [2, 4096], P(None, 'tp'), may hold values from -1.5 to 1.5
- w_down: bfloat16 [2, 1024, 4096], P(None, ('shard', 'ctx'), 'tp'), may hold values from -0.09375 to 0.09375
- b_down: bfloat16 [2, 1024], replicated, may hold values from -1.5 to 1.5
- cotangent: bfloat16 [2, 2560, 1024], P('shard', 'ctx'), may hold values from -6 to 6
Outputs:
- mixed: bfloat16 [2, 2560, 1024], P('shard', 'ctx')
- token_grads: float32 [2, 2560, 1024], P('shard', 'ctx')
- ln1_gain_grad: float32 [2, 1024], replicated
- ln1_bias_grad: float32 [2, 1024], replicated
- qkv_grad: float32 [2, 1024, 3072], P(None, ('shard', 'ctx'), 'tp')
- qv_bias_grad: float32 [2, 2048], P(None, 'tp')
- out_grad: float32 [2, 1024, 1024], P(None, ('shard', 'ctx'), 'tp')
- out_bias_grad: float32 [2, 1024], replicated
- ln2_gain_grad: float32 [2, 1024], replicated
- ln2_bias_grad: float32 [2, 1024], replicated
- up_grad: float32 [2, 1024, 4096], P(None, ('shard', 'ctx'), 'tp')
- up_bias_grad: float32 [2, 4096], P(None, 'tp')
- down_grad: float32 [2, 1024, 4096], P(None, ('shard', 'ctx'), 'tp')
- down_bias_grad: float32 [2, 1024], replicated
Inputs may be any that keep to these rules, and one draw needn't show every extreme that they name: block_tokens[i, j] live tokens stand first in the j-th block of 640 slots of image i, the rest of that block is empty; the blocks of an image hold 2048 live tokens together, and one block of each image holds exactly 640.
All inputs are finite; a program needn't handle non-finite values.
Results may differ from a plain program's by a relative error of at most 0.019.
Values may be sent and summed in bfloat16 or wider, within the bound.
A program may use at most 192 MiB of HBM per device.

v0:
```python
import functools
import math

import jax
import jax.numpy as jnp
from jax import lax
from jax.experimental import pallas as pl
from jax.experimental.pallas import tpu as pltpu
from jax.sharding import PartitionSpec as P

HEAD_DIM = 64
EPSILON = 1e-06
NEG_LARGE = -1e30
LOW = jnp.bfloat16
FULL = jnp.float32
PAD = 128
MESH = pl.DeviceIdType.MESH
VMEM = pltpu.VMEM
HBM = pltpu.HBM
SMEM = pltpu.SMEM


def bits_of(axis):
    size = lax.axis_size(axis)
    assert size & (size - 1) == 0
    return [1 << i for i in range(size.bit_length() - 1)]


def swap(value, axis, bit):
    size = lax.axis_size(axis)
    return lax.ppermute(value, axis, [(i, i ^ bit) for i in range(size)])


def side_of(axis, bit):
    return (lax.axis_index(axis) // bit) % 2


def rows_of(value, start, count, axis=0):
    return lax.dynamic_slice_in_dim(value, start, count, axis)


def halve(axis, bits, partial, total):
    offset, span, received = jnp.int32(0), total, []

    def summed(start, count):
        value = partial(start, count)
        for got, base in received:
            value = value + rows_of(got, start - base, count).astype(FULL)
        return value

    for bit in bits:
        half = span // 2
        side = side_of(axis, bit)
        got = swap(summed(offset + (1 - side) * half, half).astype(LOW), axis, bit)
        offset = offset + side * half
        received.append((got, offset))
        span = half
    return summed(offset, span)


def double(axis, bits, value):
    for bit in bits:
        got = swap(value, axis, bit)
        first = side_of(axis, bit) == 0
        value = jnp.concatenate(
            [jnp.where(first, value, got), jnp.where(first, got, value)], axis=0
        )
    return value


def total_over(axes, value):
    for axis in axes:
        for bit in bits_of(axis):
            value = value + swap(value, axis, bit)
    return value


def ring(value, by):
    count = lax.axis_size("ctx")
    return lax.ppermute(value, "ctx", [(i, (i + by) % count) for i in range(count)])


def gather_weight(piece):
    count = lax.axis_size("ctx")
    place = lax.axis_index("ctx")
    ways = lax.axis_size("shard")
    blocks = [piece] + [ring(piece, by) for by in range(1, count)]
    whole = jnp.zeros((ways * count,) + piece.shape, piece.dtype)
    me = lax.axis_index("shard")
    for by, block in enumerate(blocks):
        at = (place - by) % count
        held = [(jnp.int32(0), block)]
        for bit in bits_of("shard"):
            held = held + [(other ^ bit, swap(value, "shard", bit)) for other, value in held]
        for other, value in held:
            whole = lax.dynamic_update_index_in_dim(whole, value, (me ^ other) * count + at, 0)
    return whole.reshape((ways * count * piece.shape[0],) + piece.shape[1:]), blocks[-1]


def scatter_weight(partial, total):
    count = lax.axis_size("ctx")
    place = lax.axis_index("ctx")
    mine = halve("shard", bits_of("shard")[::-1], partial, total).astype(LOW)
    mine = mine.reshape((count, mine.shape[0] // count) + mine.shape[1:])
    value = lax.dynamic_index_in_dim(mine, place, 0, False).astype(FULL)
    for by in range(1, count):
        given = lax.dynamic_index_in_dim(mine, (place + by) % count, 0, False)
        value = value + ring(given, by).astype(FULL)
    return value


def dot(left, right, contract):
    return lax.dot_general(
        left, right, ((contract[0], contract[1]), ((), ())), preferred_element_type=FULL
    )


def turned(value):
    return value.astype(FULL).T.astype(LOW)


def normalize(rows, gain, shift):
    row_mean = jnp.mean(rows, axis=-1, keepdims=True)
    centred = rows - row_mean
    inverse = lax.rsqrt(jnp.mean(centred * centred, axis=-1, keepdims=True) + EPSILON)
    normed = centred * inverse
    return (normed * gain + shift, normed, inverse)


def normalize_back(grad_out, normed, inverse, gain):
    scaled = grad_out * gain
    mean_grad = jnp.mean(scaled, axis=-1, keepdims=True)
    mean_cross = jnp.mean(scaled * normed, axis=-1, keepdims=True)
    return inverse * (scaled - mean_grad - normed * mean_cross)


def gelu_pair(value):
    spread = 0.5 * (1.0 + lax.erf(value * (0.5**0.5)))
    slope = spread + value * jnp.exp(-0.5 * value * value) * (1.0 / math.sqrt(2.0 * math.pi))
    return (value * spread).astype(LOW), slope.astype(LOW)


class Mover:
    def __init__(self, sizes, send, recv, local):
        self.ctx_count, self.shard_count = sizes
        self.send, self.recv, self.local = send, recv, local
        self.copies, self.here = [], []
        self.arrived = set()
        self.landed = set()
        self.ctx = lax.axis_index("ctx")
        self.shard = lax.axis_index("shard")

    def go(self, source, target, **device):
        index = len(self.copies)
        assert index < self.send.shape[0]
        copy = pltpu.make_async_remote_copy(
            src_ref=source,
            dst_ref=target,
            send_sem=self.send.at[index],
            recv_sem=self.recv.at[index],
            device_id=device,
            device_id_type=MESH,
        )
        copy.start()
        self.copies.append(copy)
        return index

    def stay(self, source, target):
        index = len(self.here)
        assert index < self.local.shape[0]
        copy = pltpu.make_async_copy(source, target, self.local.at[index])
        copy.start()
        self.here.append(copy)
        return index

    def near(self, *indices):
        for index in indices:
            if index not in self.landed:
                self.landed.add(index)
                self.here[index].wait()

    def take(self, index):
        if index not in self.arrived:
            self.arrived.add(index)
            self.copies[index].wait_recv()

    def flip(self, bits):
        place = self.ctx
        if bits & 1:
            place = place + 1 - 2 * lax.rem(self.ctx, 2)
        if bits & 2:
            place = place + 2 - 4 * (self.ctx // 2)
        return place

    def on(self, by):
        return lax.rem(self.ctx + by, self.ctx_count)

    def back(self, by):
        return lax.rem(self.ctx + self.ctx_count - by, self.ctx_count)

    def settle(self):
        for index, copy in enumerate(self.copies):
            self.take(index)
            copy.wait_send()
        self.near(*range(len(self.here)))


class Gather:
    def __init__(self, mover, source, target, across=True):
        self.mover, self.source, self.target, self.across = mover, source, target, across
        self.over = []

    def start_line(self):
        mover = self.mover
        mine, there = self.source, self.block(mover.ctx)
        self.far = mover.go(mine, there, ctx=mover.flip(2))
        self.close = mover.go(mine, there, ctx=mover.flip(1))

    def start_over(self):
        mover = self.mover
        mine, there = self.source, self.block(mover.ctx)
        if self.across:
            self.over.append(mover.go(mine, there, shard=1 - mover.shard))
        self.own = mover.stay(mine, there)

    def block(self, ctx):
        mover = self.mover
        rows = self.source.shape[0]
        start = ctx * rows
        if self.across:
            start = start + mover.shard * mover.ctx_count * rows
        return self.target.at[pl.ds(pl.multiple_of(start, rows), rows)]

    def pass_on(self, stage):
        mover = self.mover
        if stage == 1:
            mover.take(self.far)
            rows = self.block(mover.flip(2))
            self.passed = mover.go(rows, rows, ctx=mover.flip(1))
        elif stage == 2:
            mover.take(self.close)
            rows = self.block(mover.flip(1))
        else:
            mover.take(self.passed)
            rows = self.block(mover.flip(3))
        if self.across:
            self.over.append(mover.go(rows, rows, shard=1 - mover.shard))

    def have(self):
        for copy in self.over:
            self.mover.take(copy)
        self.mover.near(self.own)


class Across:
    def __init__(self, mover, source, target):
        rows = source.shape[0]
        there = target.at[pl.ds(pl.multiple_of(mover.shard * rows, rows), rows)]
        self.mover = mover
        self.copy = mover.go(source, there, shard=1 - mover.shard)
        self.own = mover.stay(source, there)

    def have(self):
        self.mover.take(self.copy)
        self.mover.near(self.own)


class Reduce:
    def __init__(self, mover, buffers, out, lhs, rhs):
        self.mover, self.out, self.lhs, self.rhs = mover, out, lhs, rhs
        self.give, self.got, self.mid, self.line = buffers
        self.half = self.give.shape[0]
        self.block = self.half // mover.ctx_count

    def compute(self, target, shard):
        chunk = min(256, self.half)

        def step(i, carry):
            at = pl.ds(pl.multiple_of(shard * self.half + i * chunk, chunk), chunk)
            here = pl.ds(pl.multiple_of(i * chunk, chunk), chunk)
            target[here, :] = dot(self.lhs[:, at], self.rhs[...], ((0,), (0,))).astype(LOW)
            return carry

        lax.fori_loop(0, self.half // chunk, step, 0)

    def begin_blocks(self):
        mover = self.mover
        self.blocks = {}
        for bits in (3, 2, 1, 0):
            ctx = mover.flip(bits)
            at = pl.ds(pl.multiple_of(ctx * self.block, self.block), self.block)
            start = pl.multiple_of((1 - mover.shard) * self.half + ctx * self.block, self.block)
            lhs = self.lhs[:, pl.ds(start, self.block)]
            self.give[at, :] = dot(lhs, self.rhs[...], ((0,), (0,))).astype(LOW)
            self.blocks[bits] = mover.go(
                self.give.at[at], self.got.at[at], shard=1 - mover.shard
            )

    def own(self):
        self.compute(self.mid, self.mover.shard)

    def fold_blocks(self, *which):
        mover = self.mover
        for bits in which:
            mover.take(self.blocks[bits])
            ctx = mover.flip(bits)
            at = pl.ds(pl.multiple_of(ctx * self.block, self.block), self.block)
            self.mid[at, :] = (
                self.mid[at, :].astype(FULL) + self.got[at, :].astype(FULL)
            ).astype(LOW)

    def rows(self, ctx):
        return self.mid.at[pl.ds(pl.multiple_of(ctx * self.block, self.block), self.block)]

    def send_first(self):
        mover = self.mover
        self.first = mover.go(self.rows(mover.flip(3)), self.line.at[1], ctx=mover.flip(1))

    def send_second(self):
        mover = self.mover
        self.second = mover.go(self.rows(mover.flip(1)), self.line.at[0], ctx=mover.flip(1))

    def send_third(self):
        mover = self.mover
        mover.take(self.first)
        rows = self.rows(mover.flip(2))
        rows[...] = (rows[...].astype(FULL) + self.line[1].astype(FULL)).astype(LOW)
        self.third = mover.go(rows, self.line.at[2], ctx=mover.flip(2))

    def done(self):
        self.mover.take(self.second)
        self.mover.take(self.third)
        value = self.rows(self.mover.ctx)[...].astype(FULL)
        self.out[...] = value + self.line[0].astype(FULL) + self.line[2].astype(FULL)


def reduce_buffers(half, width, count):
    return [
        VMEM((half, width), LOW),
        VMEM((half, width), LOW),
        VMEM((half, width), LOW),
        VMEM((count - 1, half // count, width), LOW),
    ]


def greet(mover, shard):
    barrier = pltpu.get_barrier_semaphore()
    peers = [dict(ctx=mover.on(by)) for by in range(1, mover.ctx_count)]
    peers += [dict(tp=peer) for peer in tp_peers()]
    if shard:
        peers.append(dict(shard=1 - mover.shard))
    for peer in peers:
        pl.semaphore_signal(barrier, inc=1, device_id=peer, device_id_type=MESH)
    pl.semaphore_wait(barrier, len(peers))


def tp_peers():
    place = lax.axis_index("tp")
    core, far = lax.rem(place, 2), place // 2
    return place + 1 - 2 * core, place + 2 - 4 * far


def run(kernel, name, ident, inputs, outputs, scratch, remote, local, sizes, vmem, flops):
    n_in, n_out, n_scratch = len(inputs), len(outputs), len(scratch)

    def body(*refs):
        ins, outs = refs[:n_in], refs[n_in : n_in + n_out]
        work = refs[n_in + n_out :]
        mover = Mover(sizes, *work[n_scratch:])
        kernel(mover, ins, outs, work[:n_scratch])

    return pl.pallas_call(
        body,
        in_specs=[pl.BlockSpec(memory_space=space) for _, space in inputs],
        out_specs=[pl.BlockSpec(memory_space=space) for _, _, space in outputs],
        out_shape=[jax.ShapeDtypeStruct(shape, dtype) for shape, dtype, _ in outputs],
        scratch_shapes=list(scratch)
        + [
            pltpu.SemaphoreType.DMA((remote,)),
            pltpu.SemaphoreType.DMA((remote,)),
            pltpu.SemaphoreType.DMA((local,)),
        ],
        compiler_params=pltpu.CompilerParams(
            collective_id=ident, has_side_effects=True, vmem_limit_bytes=vmem * 2**20
        ),
        cost_estimate=pl.CostEstimate(flops=flops, bytes_accessed=2**24, transcendentals=0),
        name=name,
    )(*[value for value, _ in inputs])


def order_of(block, count):
    return (block + count - 1) % count


def tiles_of(count, capacity, tile):
    ends = [-(-(p + 1) * capacity // tile) for p in range(count)]
    return list(zip([0] + ends[:-1], ends))


def tile_at(t, tile):
    return pl.ds(pl.multiple_of(t * tile, tile), tile)


def turned_product(left, right, bias, target):
    value = jnp.dot(left[...], right[...], preferred_element_type=FULL)
    if bias is not None:
        value = value + bias[0:1, :]
    target[...] = turned(value.astype(LOW))


def head_rows(ref, head, width):
    return ref.at[pl.ds(pl.multiple_of(head * width, 16), width)]


def attend_part(size, tile, mover, joint, bias, heads, qkv, o_ref, lse, work, after_send, begun, between):
    k_ref, q_ref, v_ref, low_ref, score_ref, top_ref = work
    count, width, capacity = qkv.shape
    slots = count * capacity
    sent = [None] + [
        mover.go(head_rows(joint, mover.on(by), width), qkv.at[by], ctx=mover.on(by))
        for by in range(1, count)
    ]
    after_send()
    qkv[0] = head_rows(joint, mover.ctx, width)[...]
    q_ref[size:PAD, :] = jnp.concatenate(
        [jnp.ones((16, slots), LOW), jnp.zeros((PAD - size - 16, slots), LOW)], axis=0
    )

    v_ref[size : size + 16, :] = jnp.ones((16, slots), LOW)

    def prepare(r):
        here = slice(r * capacity, (r + 1) * capacity)
        p = order_of(r, count)
        q_ref[0:size, p * capacity : (p + 1) * capacity] = (
            qkv[r, 0:size, :] * (size**-0.5)
        ).astype(LOW)
        v_ref[0:size, here] = qkv[r, 2 * size : 3 * size, :]
        keys = jnp.concatenate(
            [qkv[r, size : 2 * size, :], bias[:, here], jnp.zeros((PAD - size - 16, capacity), LOW)],
            axis=0,
        )
        k_ref[here, :] = turned(keys)

    prepare(0)
    for by in range(1, count):
        mover.take(sent[by])
        prepare(by)

    begun()
    last = slots // tile - 1
    assert last % 2 == 1

    def phase(t, now, following, then):
        at, ahead = tile_at(t, tile), tile_at(following, tile)
        top = top_ref[now, 0:1, :]
        summed = jnp.zeros((size + 16, tile), FULL)
        new_top = jnp.full((1, tile), NEG_LARGE, FULL)
        for r in range(count):
            here = slice(r * capacity, (r + 1) * capacity)
            scores = jnp.dot(k_ref[here, :], q_ref[:, ahead], preferred_element_type=FULL)
            score_ref[then, here, :] = scores
            new_top = jnp.maximum(new_top, jnp.max(scores, axis=0, keepdims=True))
            weights = jnp.exp(score_ref[now, here, :] - top)
            summed = summed + jnp.dot(
                v_ref[:, here], weights.astype(LOW), preferred_element_type=FULL
            )
        top_ref[then] = jnp.broadcast_to(new_top, (8, tile))
        total = summed[size : size + 1]
        out = summed[0:size] / total
        o_ref[:, at] = out
        low_ref[:, at] = out.astype(LOW)
        lse[:, at] = jnp.broadcast_to(top + jnp.log(total), (8, tile))

    def step(i, carry):
        phase(2 * i, 0, 2 * i + 1, 1)
        phase(2 * i + 1, 1, jnp.minimum(2 * i + 2, last), 0)
        return carry

    scores = jnp.dot(k_ref[...], q_ref[:, 0:tile], preferred_element_type=FULL)
    score_ref[0] = scores
    top_ref[0] = jnp.broadcast_to(jnp.max(scores, axis=0, keepdims=True), (8, tile))
    arriving = []
    for p, (low, high) in enumerate(tiles_of(count, capacity, 2 * tile)):
        lax.fori_loop(low, high, step, 0)
        done = low_ref.at[:, p * capacity : (p + 1) * capacity]
        if p < count - 1:
            there = head_rows(heads, mover.ctx, size)
            arriving.append(mover.go(done, there, ctx=mover.back(p + 1)))
        else:
            head_rows(heads, mover.ctx, size)[...] = low_ref[:, p * capacity : (p + 1) * capacity]
        between(p + 1)
    for copy in arriving:
        mover.take(copy)


def below(row, ones):
    width = row.shape[1]
    high = row.astype(LOW).astype(FULL)
    middle = (row - high).astype(LOW).astype(FULL)
    low = row - high - middle
    lead = jnp.full((1, width), 1.0 if ones else 0.0, FULL)
    rest = jnp.zeros((PAD // 2 - 4, width), FULL)
    return jnp.concatenate([lead, high, middle, low, rest], axis=0).astype(LOW)


def attend_back_part(size, tile, mover, parts, bias, qkv, o_ref, lse, grads, work, ready, waiting, begun, between):
    k_ref, v_ref, q_ref, do_ref, nat_ref, dq_ref, dk_ref, dv_ref, got, back = work
    count, width, capacity = qkv.shape
    slots = count * capacity
    sent = [None] + [
        mover.go(head_rows(parts, mover.on(by), size), got.at[by], ctx=mover.on(by))
        for by in range(1, count)
    ]
    got[0] = head_rows(parts, mover.ctx, size)[...]
    waiting()
    ready()
    q_ref[size:PAD, :] = below(lse[0:1, :], True)
    dq_ref[...] = jnp.zeros_like(dq_ref)
    off = (lax.broadcasted_iota(jnp.int32, (16, capacity), 0) + 2) // 3
    taken = jnp.where(off == 1, -1.0, 0.0).astype(LOW)
    pad = jnp.zeros((PAD - size - 16, capacity), LOW)
    for r in range(count):
        here = slice(r * capacity, (r + 1) * capacity)
        k_ref[here, :] = turned(
            jnp.concatenate([qkv[r, size : 2 * size, :], bias[:, here] + taken, pad], axis=0)
        )
        v_ref[here, :] = turned(
            jnp.concatenate([qkv[r, 2 * size : 3 * size, :], taken, pad], axis=0)
        )
    for r in range(count):
        if r:
            mover.take(sent[r])
        p = order_of(r, count)
        at = slice(p * capacity, (p + 1) * capacity)
        scaled = (qkv[r, 0:size, :] * (size**-0.5)).astype(LOW)
        dout = got[r]
        q_ref[0:size, at] = scaled
        do_ref[0:size, at] = dout
        nat_ref[at, :] = turned(jnp.concatenate([scaled, dout], axis=0))
        delta = jnp.sum(dout.astype(FULL) * o_ref[:, at], axis=0, keepdims=True)
        do_ref[size:PAD, at] = below(delta, False)

    begun()
    tiles = tiles_of(count, capacity, tile)
    arriving = []
    mine = head_rows(grads, mover.ctx, width)
    for turn, r in enumerate(list(range(1, count)) + [0]):
        here = slice(r * capacity, (r + 1) * capacity)
        dk_ref[...] = jnp.zeros_like(dk_ref)
        dv_ref[...] = jnp.zeros_like(dv_ref)

        def step(t, carry, r=r, here=here):
            at = tile_at(t, tile)
            scores = jnp.dot(k_ref[here, :], q_ref[:, at], preferred_element_type=FULL)
            chance = jnp.exp(scores)
            chance_grad = jnp.dot(v_ref[here, :], do_ref[:, at], preferred_element_type=FULL)
            score_grad = (chance * chance_grad).astype(LOW)
            dq_ref[:, at] += jnp.dot(
                qkv[r, size : 2 * size, :], score_grad, preferred_element_type=FULL
            )
            dk_ref[...] += jnp.dot(score_grad, nat_ref[at, :], preferred_element_type=FULL)
            dv_ref[...] += jnp.dot(
                chance.astype(LOW), nat_ref[at, :], preferred_element_type=FULL
            )
            return carry

        if r:
            lax.fori_loop(0, tiles[-1][1], step, 0)
        else:
            for p, (low, high) in enumerate(tiles):
                lax.fori_loop(low, high, step, 0)
                at = slice(p * capacity, (p + 1) * capacity)
                value = (dq_ref[:, at] * (size**-0.5)).astype(LOW)
                if p < count - 1:
                    back[p + 1, 0:size, :] = value
                    arriving.append(
                        mover.go(
                            back.at[p + 1, 0:size], mine.at[0:size], ctx=mover.back(p + 1)
                        )
                    )
                else:
                    mine[0:size, :] = value
        keys = dk_ref[...].T[0:size].astype(LOW)
        values = dv_ref[...].T[size : 2 * size].astype(LOW)
        if r:
            back[r, size : 2 * size, :] = keys
            back[r, 2 * size : 3 * size, :] = values
            arriving.append(
                mover.go(
                    back.at[r, size : 3 * size], mine.at[size : 3 * size], ctx=mover.back(r)
                )
            )
        else:
            mine[size : 2 * size, :] = keys
            mine[2 * size : 3 * size, :] = values
        between(turn)
    for copy in arriving:
        mover.take(copy)


def attend_back_buffers(size, count, capacity):
    slots = count * capacity
    return [
        VMEM((slots, PAD), LOW),
        VMEM((slots, PAD), LOW),
        VMEM((PAD, slots), LOW),
        VMEM((PAD, slots), LOW),
        VMEM((slots, PAD), LOW),
        VMEM((size, slots), FULL),
        VMEM((capacity, PAD), FULL),
        VMEM((capacity, PAD), FULL),
        VMEM((count, size, capacity), LOW),
        VMEM((count, 3 * size, capacity), LOW),
    ]


class Round:
    def __init__(self, mover, rows, full, buffers):
        place = lax.axis_index("tp")
        core, far = lax.rem(place, 2), place // 2
        self.mover, self.full = mover, full
        self.give, self.ra, self.passing, self.rb, self.keep = buffers
        self.span = rows // 4
        self.half = self.span // 2
        self.mate, self.far = tp_peers()

        def quarter(c, f):
            return (c * 2 + f) * self.span

        self.own, self.other = quarter(core, far), quarter(core, 1 - far)
        self.mate_own, self.mate_other = quarter(1 - core, far), quarter(1 - core, 1 - far)

    def rows(self, start, count=None):
        return pl.ds(pl.multiple_of(start, 16), count or self.span)

    def hand(self, slot, value):
        self.give[slot] = value.astype(LOW)
        return self.mover.go(self.give.at[slot], self.ra.at[slot], tp=self.mate)

    def onward(self, value, index):
        self.mover.take(index)
        self.passing[...] = (value + self.ra[1].astype(FULL)).astype(LOW)
        return [
            self.mover.go(self.passing.at[at], self.rb.at[at], tp=self.far)
            for at in (pl.ds(0, self.half), pl.ds(self.half, self.half))
        ]

    def close(self, far_copies, index, finish, halfway=None):
        self.mover.take(index)
        self.keep[...] += self.ra[0].astype(FULL)
        self.to_far, self.to_mate = [], []
        for c in range(2):
            at = pl.ds(c * self.half, self.half)
            self.mover.take(far_copies[c])
            low = finish(at, self.keep[at] + self.rb[at].astype(FULL))
            mine = self.full.at[self.rows(self.own + c * self.half, self.half)]
            mine[...] = low
            self.to_far.append(self.mover.go(mine, mine, tp=self.far))
            self.to_mate.append(self.mover.go(mine, mine, tp=self.mate))
            if halfway and c == 0:
                halfway()

    def eager(self, make, finish, meanwhile=None, halfway=None):
        first = self.hand(1, make(self.mate_other))
        copies = self.onward(make(self.other), first)
        second = self.hand(0, make(self.mate_own))
        self.keep[...] = make(self.own)
        if meanwhile:
            meanwhile()
        self.close(copies, second, finish, halfway)

    def after(self, before, make, finish, meanwhile, between):
        before.have_mate_own()
        second = self.hand(0, make(self.mate_own))
        self.keep[...] = make(self.own)
        before.have_other()
        between()
        value = make(self.other)
        before.have_mate_other()
        first = self.hand(1, make(self.mate_other))
        copies = self.onward(value, first)
        meanwhile()
        self.close(copies, second, finish)

    def have_mate_own(self):
        for copy in self.to_mate:
            self.mover.take(copy)

    def have_other(self):
        self.passed = []
        for c in range(2):
            self.mover.take(self.to_far[c])
            rows = self.full.at[self.rows(self.other + c * self.half, self.half)]
            self.passed.append(self.mover.go(rows, rows, tp=self.mate))

    def have_mate_other(self):
        for copy in self.passed:
            self.mover.take(copy)

    def have(self):
        self.have_mate_own()
        self.have_other()
        self.have_mate_other()


ROUND_COPIES = 10


def round_buffers(rows, width):
    span = rows // 4
    return [
        VMEM((2, span, width), LOW),
        VMEM((2, span, width), LOW),
        VMEM((span, width), LOW),
        VMEM((span, width), LOW),
        VMEM((span, width), FULL),
    ]


NAMES = ("qkv", "out", "up", "down")


def layer_kernel(plan, last, size, tile, mover, ins, outs, work):
    ins, outs, work = iter(ins), iter(outs), iter(work)
    source = next(ins)
    x_ref = None if plan.entry else next(ins)
    live_ref = next(ins)
    far_params = [next(ins) for _ in range(8)]
    stream, following = next(outs), next(outs)
    far_qkv, far_o, far_lse, far_heads, far_middle, far_second, far_hidden, far_slope = [
        next(outs) for _ in range(8)
    ]
    far_first = next(outs) if plan.entry else None
    joint, nat, heads, qkv, o_ref, lse, middle, second, hidden, slope = [
        next(work) for _ in range(10)
    ]
    first = next(work) if plan.entry else source
    attend_work = [next(work) for _ in range(6)]
    one_work, two_work = [next(work) for _ in range(5)], [next(work) for _ in range(5)]
    rows = source.shape[0]
    bias, qkv_bias = next(work), next(work)
    params = [next(work) for _ in range(8)]
    whole = {name: next(work) for name in NAMES}
    gathers, loads = {}, {}
    for name in plan.held:
        loads[name] = (next(ins), whole[name])
    half_refs = {name: next(ins) for name in plan.halves}
    for name in plan.own:
        gathers[name, 0] = Gather(mover, next(ins).at[plan.layer], whole[name])
    kept_ahead = {name: next(outs) for name in plan.ahead + plan.lines}
    for name in plan.ahead + plan.lines:
        gathers[name, 1] = Gather(
            mover, next(ins).at[plan.layer + 1], next(work), name in plan.ahead
        )
    kept = {name: next(outs) for name in plan.kept}

    greet(mover, bool(gathers))
    halves = {name: Across(mover, half_refs[name], whole[name]) for name in plan.halves}
    if plan.entry:
        gathers_first = [key for key in [("qkv", 0)] if key in gathers]
        for key in gathers_first:
            gathers[key].start_line()
            gathers[key].start_over()
    param_loads = [mover.stay(there, here) for there, here in zip(far_params, params)]
    waiting_loads = dict(loads)
    loads = {}

    def load(names):
        for name in names:
            if name in waiting_loads and name not in loads:
                loads[name] = mover.stay(*waiting_loads[name])

    load(["qkv"])

    def have(name):
        if name in waiting_loads:
            mover.near(loads[name])
            load(NAMES)
        else:
            (halves[name] if name in halves else gathers[name, 0]).have()
            mover.stay(whole[name], kept[name])
        return whole[name]

    def begin(keys):
        for key in keys:
            if key in gathers:
                gathers[key].start_line()

    def begin_over(keys):
        for key in keys:
            if key in gathers:
                gathers[key].start_over()

    def pass_on(keys, stage):
        for key in keys:
            if key in gathers:
                gathers[key].pass_on(stage)

    def pass_all(keys):
        for stage in (1, 2, 3):
            pass_on(keys, stage)

    mover.near(*param_loads)
    layer, after = plan.layer, min(plan.layer + 1, params[0].shape[0] - 1)

    def row(index, layer=layer):
        return params[index][...].astype(FULL)[layer : layer + 1]

    b_out, gain2, shift2, b_down, b_up = row(0), row(1), row(2), row(3), row(6)
    gain1, shift1, gain0, shift0 = row(4, after), row(5, after), row(4), row(5)
    qkv_bias[...] = joint_bias(row(7), size, joint.shape[0])
    key_bias(mover, live_ref, bias)
    ahead, lines = [("qkv", 1)], [("out", 1), ("up", 1)]
    one = Round(mover, rows, second, one_work)
    two = Round(mover, rows, following, two_work)
    if plan.entry:
        chunk = rows // 5 if rows % 80 == 0 else rows

        def norm_step(i, carry):
            at = pl.ds(pl.multiple_of(i * chunk, 16), chunk)
            value = normalize(source[at, :].astype(FULL), gain0, shift0)[0]
            first[at, :] = value.astype(LOW)
            return carry

        lax.fori_loop(0, rows // chunk, norm_step, 0)
        mover.stay(first, far_first)
        pass_all([("qkv", 0)])
        begin([("out", 0), ("up", 0)])
        begin_over([("out", 0), ("up", 0), ("down", 0)] + ahead + lines)
        turned_product(first, have("qkv"), qkv_bias, joint)
    else:
        turned_product(first, have("qkv"), qkv_bias, joint)

    def after_send():
        if plan.entry:
            pass_all([("out", 0), ("up", 0)])
        else:
            for name in plan.own:
                gathers[name, 0].start_over()

    def begun():
        begin([("down", 0)])

    def between(p):
        if p > 2:
            pass_on([("down", 0)], p - 2)
        if p == 4:
            if not plan.entry:
                begin_over(ahead + lines)
            begin(ahead)

    attend_part(
        size, tile, mover, joint, bias, heads, qkv, o_ref, lse, attend_work, after_send, begun, between
    )
    nat[...] = turned(heads[...])
    w_out = have("out")

    def out_part(start):
        return dot(nat[one.rows(start), :], w_out[...], ((1,), (1,)))

    def to_second(at, value):
        if plan.entry:
            before = source[one.rows(one.own + at.start, at.size), :].astype(FULL)
        else:
            before = x_ref[at]
        value = before + value + b_out
        middle[at] = value
        return normalize(value, gain2, shift2)[0].astype(LOW)

    def meanwhile():
        mover.stay(qkv, far_qkv)
        mover.stay(o_ref, far_o)
        mover.stay(lse, far_lse)
        mover.stay(nat, far_heads)
        pass_on([("down", 0)], 3)

    one.eager(out_part, to_second, meanwhile, lambda: pass_on(ahead, 1))
    pass_on(ahead, 2)
    begin(lines)
    w_up, w_down = have("up"), have("down")

    def mlp_part(start):
        at = two.rows(start)
        pre = jnp.dot(second[at, :], w_up[...], preferred_element_type=FULL) + b_up
        low, low_slope = gelu_pair(pre)
        hidden[at, :] = low
        slope[at, :] = low_slope
        return dot(low, w_down[...], ((1,), (1,)))

    def to_following(at, value):
        value = middle[at] + value + b_down
        stream[at] = value
        if last:
            return live_rows(value, two.own + at.start, live_ref[0, mover.ctx]).astype(LOW)
        return normalize(value, gain1, shift1)[0].astype(LOW)

    def meanwhile():
        mover.stay(middle, far_middle)
        mover.stay(second, far_second)
        mover.stay(hidden, far_hidden)
        mover.stay(slope, far_slope)
        pass_on(lines, 1)

    two.after(one, mlp_part, to_following, meanwhile, lambda: pass_on(ahead, 3))
    two.have()
    pass_on(lines, 2)
    pass_on(lines, 3)
    for name in plan.ahead + plan.lines:
        gathers[name, 1].have()
        mover.stay(gathers[name, 1].target, kept_ahead[name])
    mover.settle()


class Plan:
    def __init__(self, layer, last, inside):
        self.layer, self.entry = layer, layer == 0
        self.own = (NAMES if layer == 0 else ("down",)) if inside else ()
        self.halves = ("out", "up") if inside and layer else ()
        self.ahead = ("qkv",) if inside and not last else ()
        self.lines = ("out", "up") if inside and not last else ()
        self.kept = self.own + self.halves
        self.held = tuple(name for name in NAMES if name not in self.kept)


def forward_layer(source, x, live, params, gathered, weights, plan, last, size, sizes, ident):
    rows, width = source.shape
    count = sizes[0]
    joint, hidden = weights["qkv"].shape[2], weights["up"].shape[2]
    heads = joint // (3 * size)
    attn, slots, span = heads * size, count * rows, rows // 4
    tile = 256 if slots % 256 == 0 else PAD
    columns = {"qkv": joint, "out": attn, "up": hidden, "down": hidden}
    inputs = [(source, VMEM)] + ([] if plan.entry else [(x, VMEM)])
    inputs += [(live, SMEM)] + [(value, HBM) for value in params]
    inputs += [(gathered[name, plan.layer], HBM) for name in plan.held]
    inputs += [(gathered[name, plan.layer, 0], HBM) for name in plan.halves]
    inputs += [(weights[name], HBM) for name in plan.own + plan.ahead + plan.lines]
    saved = [
        ((count, 3 * size, rows), LOW),
        ((size, slots), FULL),
        ((8, slots), FULL),
        ((rows, attn), LOW),
        ((span, width), FULL),
        ((rows, width), LOW),
        ((rows, hidden), LOW),
        ((rows, hidden), LOW),
    ]
    outputs = [((span, width), FULL, VMEM), ((rows, width), LOW, VMEM)]
    outputs += [(shape, dtype, HBM) for shape, dtype in saved]
    if plan.entry:
        outputs.append(((rows, width), LOW, HBM))
    ahead = [(width, columns[name]) for name in plan.ahead]
    ahead += [(width // 2, columns[name]) for name in plan.lines]
    outputs += [(shape, LOW, HBM) for shape in ahead]
    outputs += [((width, columns[name]), LOW, HBM) for name in plan.kept]
    qkv_shape, o_shape, lse_shape, heads_shape = saved[:4]
    scratch = [VMEM((joint, rows), LOW), VMEM((rows, attn), LOW), VMEM((attn, rows), LOW)]
    scratch += [VMEM(*pair) for pair in saved[:3] + saved[4:]]
    if plan.entry:
        scratch.append(VMEM((rows, width), LOW))
    scratch += [
        VMEM((slots, PAD), LOW),
        VMEM((PAD, slots), LOW),
        VMEM((size + 16, slots), LOW),
        VMEM((size, slots), LOW),
        VMEM((2, slots, tile), FULL),
        VMEM((2, 8, tile), FULL),
    ]
    scratch += round_buffers(rows, width) + round_buffers(rows, width)
    scratch += [VMEM((16, slots), LOW), VMEM((16, joint), FULL)]
    scratch += [VMEM(value.shape, value.dtype) for value in params]
    scratch += [VMEM((width, columns[name]), LOW) for name in NAMES]
    scratch += [VMEM(shape, LOW) for shape in ahead]
    results = run(
        functools.partial(layer_kernel, plan, last, size, tile),
        "forward_layer",
        ident,
        inputs,
        outputs,
        scratch,
        2 * (count - 1) + 2 * ROUND_COPIES + 2 * count * len(plan.kept + plan.ahead + plan.lines),
        10 + 2 * len(plan.kept + plan.ahead + plan.lines) + len(plan.held) + len(params),
        sizes,
        58,
        2 * rows * width * (2 * hidden + attn + joint) + 4 * slots * slots * 256,
    )
    stream, following = results[:2]
    kept = results[2 : 11 if plan.entry else 10]
    rest = iter(results[2 + len(kept) :])
    for name in plan.ahead:
        gathered[name, plan.layer + 1] = next(rest)
    for name in plan.lines:
        gathered[name, plan.layer + 1, 0] = next(rest)
    for name in plan.kept:
        gathered[name, plan.layer] = next(rest)
    return stream, following, kept


class SmallSums:
    def __init__(self, mover, rows, held, got):
        self.mover, self.rows, self.held, self.got = mover, rows, held, got
        self.stage = 0
        mate, far = tp_peers()
        self.peers = [
            dict(tp=mate),
            dict(tp=far),
            dict(shard=1 - mover.shard),
            dict(ctx=mover.flip(2)),
            dict(ctx=mover.flip(1)),
        ]

    def part(self, stage):
        return pl.ds(0, self.rows if stage < 2 else self.held.shape[1])

    def step(self):
        stage, mover = self.stage, self.mover
        if stage:
            mover.take(self.copy)
            at = self.part(stage - 1)
            self.held[stage] = self.held[stage - 1]
            self.held[stage, at, :] = self.held[stage - 1, at, :] + self.got[stage - 1, at, :]
        if stage < len(self.peers):
            at = self.part(stage)
            self.copy = mover.go(
                self.held.at[stage, at], self.got.at[stage, at], **self.peers[stage]
            )
        self.stage = stage + 1

    def value(self):
        return self.held[len(self.peers)]


def key_bias(mover, live_ref, bias):
    capacity = bias.shape[1] // mover.ctx_count
    row = lax.broadcasted_iota(jnp.int32, (16, capacity), 0)
    slot = lax.broadcasted_iota(jnp.int32, (16, capacity), 1)
    for r in range(mover.ctx_count):
        live = live_ref[0, mover.back(r)]
        value = jnp.where((row == 0) & (slot >= live), NEG_LARGE, 0.0)
        bias[:, r * capacity : (r + 1) * capacity] = value.astype(LOW)


def pair_columns(rows, width, size, turn):
    shape = (width, rows) if turn else (rows, width)
    given = lax.broadcasted_iota(jnp.int32, shape, 1 if turn else 0)
    column = lax.broadcasted_iota(jnp.int32, shape, 0 if turn else 1)
    head, within = column // (3 * size), column % (3 * size)
    wanted = head * (2 * size) + jnp.where(within < size, within, within - size)
    key = (within >= size) & (within < 2 * size)
    return jnp.where((given == wanted) & ~key, 1.0, 0.0).astype(LOW)


def joint_bias(pair, size, width):
    rows = pair.shape[1]
    spread = jnp.broadcast_to(pair, (16, rows)).astype(LOW)
    return jnp.dot(spread, pair_columns(rows, width, size, False), preferred_element_type=FULL)


def live_rows(value, start, live):
    row = start + lax.broadcasted_iota(jnp.int32, value.shape, 0)
    return jnp.where(row < live, value, 0.0)


def sums_into(sums, first, at, values):
    for index, value in enumerate(values):
        row = first + index
        added = jnp.sum(value, axis=0, keepdims=True)
        width = added.shape[1]
        sums[row : row + 1, 0:width] = (
            added if at.start == 0 else sums[row : row + 1, 0:width] + added
        )


def back_kernel(plan, size, tile, mover, ins, outs, work):
    ins, outs, work = iter(ins), iter(outs), iter(work)
    source = next(ins)
    x_ref = None if plan.last else next(ins)
    live_ref, far_gain2, far_gain1 = [next(ins) for _ in range(3)]
    far = [next(ins) for _ in range(14)]
    late_far = next(ins) if plan.late else None
    others = [(next(ins), next(ins)) for _ in range(plan.others)]
    stream, following = next(outs), next(outs)
    grad_outs = {name: next(outs) for name in NAMES if plan.inside and (name != "qkv" or plan.final)}
    mid_out = next(outs) if plan.inside and not plan.final else None
    late_out = next(outs) if plan.late else None
    split = local = totals = None
    if plan.joined:
        totals = next(outs)
    else:
        split, local = next(outs), next(outs)
    wholes = {} if plan.inside else {name: next(outs) for name in NAMES}
    near = [next(work) for _ in range(14)]
    slope, w_down, w_up, middle, hidden, second, w_out, heads, qkv, o_ref, lse, first, w_qkv, before = near
    grad = next(work) if plan.last else source
    pre_grad, attn_grad, parts, grads, nat = [next(work) for _ in range(5)]
    attend_work = [next(work) for _ in range(10)]
    one_work, two_work = [next(work) for _ in range(5)], [next(work) for _ in range(5)]
    rows, width = source.shape
    reduces = {}
    if plan.inside:
        pairs = {
            "down": (grad, hidden),
            "up": (second, pre_grad),
            "out": (attn_grad, heads),
            "qkv": (first, nat),
        }
        for name in ("down", "up", "out", "qkv"):
            buffers = [next(work) for _ in range(4)]
            reduces[name] = Reduce(mover, buffers, grad_outs.get(name), *pairs[name])
    late = None
    if plan.late:
        late_mid, late_line = next(work), next(work)
        late = Reduce(mover, (late_mid, None, late_mid, late_line), late_out, None, None)
    bias, gain2_ref, gain1_ref = [next(work) for _ in range(3)]
    if plan.joined:
        split, local = next(work), next(work)
        early_held, early_got, late_held, late_got = [next(work) for _ in range(4)]
        tops = 8 * (plan.others + 1)
        early = SmallSums(mover, tops, early_held, early_got)
        final = SmallSums(mover, 8, late_held, late_got)
        everything = [(split, local)] + others

    greet(mover, plan.inside)
    gain_loads = [mover.stay(far_gain2, gain2_ref), mover.stay(far_gain1, gain1_ref)]
    one = Round(mover, rows, attn_grad, one_work)
    two = Round(mover, rows, following, two_work)
    if plan.final:
        far[13] = far[13].at[two.rows(two.own)]
    load = {index: mover.stay(far[index], near[index]) for index in (0, 1, 2)}
    if late:
        mover.near(mover.stay(late_far, late_mid))
        late.send_first()
        late.send_second()
    if plan.last:
        chunk = rows // 5 if rows % 80 == 0 else rows

        def mask_step(i, carry):
            at = pl.ds(pl.multiple_of(i * chunk, 16), chunk)
            value = source[at, :].astype(FULL)
            grad[at, :] = live_rows(value, i * chunk, live_ref[0, mover.ctx]).astype(LOW)
            return carry

        lax.fori_loop(0, rows // chunk, mask_step, 0)
    key_bias(mover, live_ref, bias)
    mover.near(*gain_loads)
    gain2, gain1 = [
        ref[...].astype(FULL)[plan.layer : plan.layer + 1] for ref in (gain2_ref, gain1_ref)
    ]
    split[...] = jnp.zeros_like(split)
    local[...] = jnp.zeros_like(local)
    split[5:6, 0:width] = jnp.sum(
        grad[one.rows(one.own), :].astype(FULL), axis=0, keepdims=True
    )
    hidden_width = slope.shape[1]

    def mlp_part(start):
        at = one.rows(start)
        pre = jnp.dot(grad[at, :], w_down[...], preferred_element_type=FULL)
        low = (pre * slope[at, :].astype(FULL)).astype(LOW)
        pre_grad[at, :] = low
        local[0:1, 0:hidden_width] += jnp.sum(low.astype(FULL), axis=0, keepdims=True)
        return dot(low, w_up[...], ((1,), (1,)))

    def to_attn(at, value):
        if plan.last:
            above = grad[one.rows(one.own + at.start, at.size), :].astype(FULL)
        else:
            above = x_ref[at]
        _, normed, inverse = normalize(middle[at], 1.0, 0.0)
        result = above + normalize_back(value, normed, inverse, gain2)
        stream[at] = result
        low = result.astype(LOW)
        sums_into(split, 2, at, (value * normed, value, low.astype(FULL)))
        return low

    def reduce(name):
        if name in reduces:
            reduces[name].begin_blocks()

    def own(name):
        if name in reduces:
            reduces[name].own()

    def first_step(name):
        if name in reduces:
            reduces[name].fold_blocks(3)
            reduces[name].send_first()

    def second_step(name):
        if name in reduces:
            reduces[name].fold_blocks(2)
            reduces[name].send_third()

    def rest(name):
        if name in reduces:
            reduces[name].fold_blocks(1)
            reduces[name].send_second()
            reduces[name].fold_blocks(0)

    def begin_early():
        if plan.joined:
            early_held[0] = jnp.zeros(early_held.shape[1:], FULL)
            for layer, (some, more) in enumerate(everything):
                first_row = 0 if layer else 2
                for row in range(first_row, 6):
                    at = row * len(everything) + layer
                    early_held[0, at : at + 1, :] = some[row : row + 1, :]
                for row in range(2 if layer else 1):
                    at = tops + row * len(everything) + layer
                    early_held[0, at : at + 1, :] = more[row : row + 1, :]

    def early_step():
        if plan.joined:
            early.step()

    def start_down():
        mover.near(load[3], load[4])
        reduce("down")
        if late:
            late.send_third()

    mover.near(load[0], load[1], load[2])
    for index in range(3, len(far)):
        load[index] = mover.stay(far[index], near[index])
    one.eager(mlp_part, to_attn, start_down)
    mover.near(load[5])
    reduce("up")
    one.have()
    mover.near(load[6])
    turned_product(attn_grad, w_out, None, parts)

    def waiting():
        begin_early()
        early_step()
        own("down")
        first_step("down")
        mover.near(load[7])
        reduce("out")
        own("out")

    def ready():
        own("up")
        mover.near(load[8], load[9], load[10])

    def between(turn):
        if turn == 0:
            early_step()
        if turn == 3:
            second_step("down")
            first_step("up")
            rest("down")

    attend_back_part(
        size,
        tile,
        mover,
        parts,
        bias,
        qkv,
        o_ref,
        lse,
        grads,
        attend_work,
        ready,
        waiting,
        lambda: None,
        between,
    )
    early_step()
    nat[...] = turned(grads[...])
    pairs_width = nat.shape[1] // 3 * 2
    picked = jnp.dot(
        nat[...], pair_columns(pairs_width, nat.shape[1], size, True), preferred_element_type=FULL
    )
    local[1:2, 0:pairs_width] = jnp.sum(picked, axis=0, keepdims=True)
    mover.near(*[load[index] for index in range(11, len(far))])

    def qkv_part(start):
        return dot(nat[two.rows(start), :], w_qkv[...], ((1,), (1,)))

    def to_following(at, value):
        row = before[at, :].astype(FULL)
        _, normed, inverse = normalize(row, 1.0, 0.0)
        result = stream[at] + normalize_back(value, normed, inverse, gain1)
        stream[at] = result
        low = result.astype(LOW)
        sums_into(split, 0, at, (value * normed, value))
        return low

    def meanwhile():
        own("qkv")
        second_step("up")
        first_step("out")
        rest("up")
        early_step()

    def halfway():
        if plan.inside:
            reduces["qkv"].fold_blocks(3)
            if plan.final:
                reduces["qkv"].send_first()

    reduce("qkv")
    two.eager(qkv_part, to_following, meanwhile, halfway)
    if plan.joined:
        late_held[0, 0:8, :] = jnp.zeros((8, late_held.shape[2]), FULL)
        late_held[0, 0:2, :] = split[0:2, :]
        late_held[0, 8:16, :] = local[...]
        final.step()
        final.step()
    two.have_mate_own()
    two.have_other()
    if plan.joined:
        final.step()
        early_step()
    second_step("out")
    rest("out")
    if plan.joined:
        final.step()
    if plan.inside:
        last = reduces["qkv"]
        if plan.final:
            second_step("qkv")
            rest("qkv")
        else:
            last.fold_blocks(2, 1, 0)
            mover.stay(last.mid, mid_out)
    two.have_mate_other()
    if plan.joined:
        final.step()
    for name in ("down", "up", "out"):
        if name in reduces:
            reduces[name].done()
    if late:
        late.done()
    if plan.inside and plan.final:
        reduces["qkv"].done()
    if plan.joined:
        final.step()
        early.step()
        totals[...] = early.value()
        last_value = final.value()
        for row in range(2):
            at = row * len(everything)
            totals[at : at + 1, :] = last_value[row : row + 1, :]
        at = tops + len(everything)
        totals[at : at + 1, :] = last_value[9:10, :]
    if not plan.inside:
        for name, (lhs, rhs) in {
            "down": (grad, hidden),
            "up": (second, pre_grad),
            "out": (attn_grad, heads),
            "qkv": (first, nat),
        }.items():
            full = Reduce(mover, (wholes[name],) * 4, None, lhs, rhs)
            full.compute(wholes[name], 0)
    mover.settle()


def gather_outputs_kernel(layers, *refs):
    count = layers * len(NAMES)
    parts, token_grads, mixed, totals = refs[:count], refs[count], refs[count + 1], refs[count + 2]
    outs, work = refs[count + 3 : count + 17], refs[count + 17 : -2]
    into, out_of = refs[-2:]
    coming, going = [], []
    pairs = [(mixed, work[4], outs[4].at[0])]
    for index in range(len(NAMES)):
        for layer in range(layers):
            pairs.append(
                (parts[index * layers + layer], work[index].at[layer], outs[index].at[layer])
            )
    for i, (source, stage, _) in enumerate(pairs):
        coming.append(pltpu.make_async_copy(source, stage, into.at[i]))
        coming[-1].start()
    outs[5][0] = token_grads[...].astype(FULL)
    for row, out in enumerate(outs[6:12]):
        out[...] = totals[row * layers : (row + 1) * layers, 0 : out.shape[1]]
    for row, out in enumerate(outs[12:14]):
        row = row + 8
        out[...] = totals[row * layers : (row + 1) * layers, 0 : out.shape[1]]
    for i, (_, stage, target) in enumerate(pairs):
        coming[i].wait()
        going.append(pltpu.make_async_copy(stage, target, out_of.at[i]))
        going[-1].start()
    for copy in going:
        copy.wait()


def gather_outputs(done, token_grads, mixed, totals, layers, widths):
    rows, width = token_grads.shape
    parts = [done[name, layer] for name in NAMES for layer in range(layers)]
    hbm, whole = pl.BlockSpec(memory_space=HBM), lambda shape: pl.BlockSpec(
        shape, lambda i: (0,) * len(shape)
    )
    shapes = [(layers,) + done[name, 0].shape for name in NAMES] + [(1, rows, width)] * 2
    types = [FULL] * 4 + [LOW, FULL]
    small = [(layers, width)] * 6 + [(layers, count) for count in widths]
    copies = len(parts) + 1
    return pl.pallas_call(
        functools.partial(gather_outputs_kernel, layers),
        grid=(1,),
        in_specs=[hbm] * len(parts) + [whole(token_grads.shape), hbm, whole(totals.shape)],
        out_specs=[hbm] * 5 + [whole(shape) for shape in shapes[5:] + small],
        out_shape=[jax.ShapeDtypeStruct(*pair) for pair in zip(shapes, types)]
        + [jax.ShapeDtypeStruct(shape, FULL) for shape in small],
        scratch_shapes=[VMEM(shape, FULL) for shape in shapes[:4]]
        + [VMEM((rows, width), LOW)]
        + [pltpu.SemaphoreType.DMA((copies,)), pltpu.SemaphoreType.DMA((copies,))],
        compiler_params=pltpu.CompilerParams(vmem_limit_bytes=60 * 2**20),
        name="gather_outputs",
    )(*parts, token_grads, mixed, totals)


class BackPlan:
    def __init__(self, layer, layers, inside):
        self.inside, self.layer = inside, layer
        self.last, self.final = layer == layers - 1, layer == 0
        self.late = inside and not self.last
        self.joined = inside and self.final
        self.others = layers - 1 if self.joined else 0


def back_layer(source, x, live, gain2, gain1, saved, late, others, plan, size, sizes, ident):
    rows, width = source.shape
    count = sizes[0]
    slope, w_down, w_up = saved[:3]
    hidden, joint, attn = slope.shape[1], saved[12].shape[1], saved[6].shape[1]
    slots, span = count * rows, rows // 4
    tile = 512 if slots % 512 == 0 else PAD
    wide = max(width, hidden, joint)
    half = width // 2
    block = half // count
    columns = {"qkv": joint, "out": attn, "up": hidden, "down": hidden}
    inputs = [(source, VMEM)] + ([] if plan.last else [(x, VMEM)])
    inputs += [(live, SMEM), (gain2, HBM), (gain1, HBM)]
    inputs += [(value, HBM) for value in saved]
    if plan.late:
        inputs.append((late, HBM))
    for pair in others[: plan.others]:
        inputs += [(value, VMEM) for value in pair]
    outputs = [((span, width), FULL, VMEM), ((rows, width), LOW, VMEM)]
    names = [name for name in NAMES if plan.inside and (name != "qkv" or plan.final)]
    outputs += [((block, columns[name]), FULL, VMEM) for name in names]
    if plan.inside and not plan.final:
        outputs.append(((half, joint), LOW, HBM))
    if plan.late:
        outputs.append(((block, joint), FULL, VMEM))
    depth = 8 * (plan.others + 1)
    if plan.joined:
        outputs.append(((depth + 8, wide), FULL, VMEM))
    else:
        outputs += [((8, wide), FULL, VMEM)] * 2
    if not plan.inside:
        outputs += [((width, columns[name]), LOW, VMEM) for name in NAMES]
    scratch = [VMEM(value.shape, value.dtype) for value in saved]
    scratch[13] = VMEM((span, width), saved[13].dtype)
    if plan.last:
        scratch.append(VMEM((rows, width), LOW))
    scratch += [
        VMEM((rows, hidden), LOW),
        VMEM((rows, width), LOW),
        VMEM((attn, rows), LOW),
        VMEM((joint, rows), LOW),
        VMEM((rows, joint), LOW),
    ]
    scratch += attend_back_buffers(size, count, rows)
    scratch += round_buffers(rows, width) + round_buffers(rows, width)
    if plan.inside:
        for name in ("down", "up", "out", "qkv"):
            scratch += reduce_buffers(half, columns[name], count)
    if plan.late:
        scratch += [VMEM((half, joint), LOW), VMEM((count - 1, block, joint), LOW)]
    scratch.append(VMEM((16, slots), LOW))
    scratch += [VMEM(value.shape, value.dtype) for value in (gain2, gain1)]
    assert 2 * (plan.others + 1) <= 8
    if plan.joined:
        scratch += [VMEM((8, wide), FULL)] * 2
        scratch += [
            VMEM((6, depth + 8, wide), FULL),
            VMEM((5, depth + 8, wide), FULL),
            VMEM((6, 16, wide), FULL),
            VMEM((5, 16, wide), FULL),
        ]
    results = run(
        functools.partial(back_kernel, plan, size, tile),
        "back_layer",
        ident,
        inputs,
        outputs,
        scratch,
        3 * (count - 1) + 2 * ROUND_COPIES + 8 * count + 10 + count,
        len(saved) + 4,
        sizes,
        58,
        6 * rows * width * (2 * hidden + attn + joint) + 10 * slots * slots * 256,
    )
    return results[:2], names, results[2:]


def shards(
    tokens,
    block_tokens,
    ln1_gain,
    ln1_bias,
    w_qkv,
    b_qv,
    w_out,
    b_out,
    ln2_gain,
    ln2_bias,
    w_up,
    b_up,
    w_down,
    b_down,
    cotangent,
):
    images, capacity, width = tokens.shape
    assert images == 1
    layers = w_qkv.shape[0]
    size = HEAD_DIM
    ctx_count = lax.axis_size("ctx")
    ctx_place = lax.axis_index("ctx")
    joint_width = w_qkv.shape[2]
    heads = joint_width // (3 * size)
    assert heads == ctx_count
    attn_width = heads * size
    hidden_width = w_up.shape[2]
    weights = {"qkv": w_qkv, "out": w_out, "up": w_up, "down": w_down}
    sizes = (ctx_count, lax.axis_size("shard"))
    inside = sizes == (4, 2)
    gathered = {}
    if not inside:
        for name, value in weights.items():
            for layer in range(layers):
                gathered[name, layer] = gather_weight(value[layer])[0]
    source, stream = tokens[0], None
    saved = []
    for layer in range(layers):
        last = layer == layers - 1
        result, following, kept = forward_layer(
            source,
            stream,
            block_tokens,
            (b_out, ln2_gain, ln2_bias, b_down, ln1_gain, ln1_bias, b_up, b_qv),
            gathered,
            weights,
            Plan(layer, last, inside),
            last,
            size,
            sizes,
            1 + layer,
        )
        before = stream if layer else source
        first = source if layer else kept[8]
        saved.append((before, first) + tuple(kept[:8]))
        source, stream = following, result
    mixed = source

    done, packs = {}, {}
    source, stream, late = cotangent[0], None, None
    for layer in reversed(range(layers)):
        before, first, qkv, head_out, lse, heads_low, middle, second, hidden, slope = saved[layer]
        plan = BackPlan(layer, layers, inside)
        whole = {name: gathered[name, layer] for name in NAMES}
        near = [slope, whole["down"], whole["up"], middle, hidden, second, whole["out"]]
        near += [heads_low, qkv, head_out, lse, first, whole["qkv"], before]
        others = [packs[key] for key in sorted(packs)]
        (stream, source), names, rest = back_layer(
            source, stream, block_tokens, ln2_gain, ln1_gain, near, late, others, plan, size, sizes, 1 + layers + layer
        )
        rest = iter(rest)
        for name in names:
            done[name, layer] = next(rest)
        if plan.inside and not plan.final:
            late = next(rest)
        if plan.late:
            done["qkv", layer + 1] = next(rest)
        if plan.joined:
            totals = next(rest)
        else:
            packs[layer] = (next(rest), next(rest))
        if not inside:
            for name in NAMES:
                value = next(rest)
                done[name, layer] = scatter_weight(
                    lambda start, count, value=value: rows_of(value, start, count).astype(FULL),
                    width,
                )
    if not inside:
        split = total_over(("tp",), jnp.stack([packs[l][0] for l in range(layers)], axis=1))
        local = jnp.stack([packs[l][1] for l in range(layers)], axis=1)
        totals = total_over(("shard", "ctx"), jnp.concatenate([split, local[:2]]))
        totals = totals.reshape(10 * layers, -1)
    pairs = b_qv.shape[1]
    outs = gather_outputs(done, source, mixed, totals, layers, (hidden_width, pairs))
    g_qkv, g_out, g_up, g_down, mixed, token_grads = outs[:6]
    g_ln1_gain, g_ln1_bias, g_ln2_gain, g_ln2_bias, g_b_out, g_b_down, g_b_up, g_b_qv = outs[6:]
    return (
        mixed,
        token_grads,
        g_ln1_gain,
        g_ln1_bias,
        g_qkv,
        g_b_qv,
        g_out,
        g_b_out,
        g_ln2_gain,
        g_ln2_bias,
        g_up,
        g_b_up,
        g_down,
        g_b_down,
    )


def solution(mesh):
    split_rows = P(None, ("shard", "ctx"), "tp")
    split_tokens = P("shard", "ctx", None)
    return jax.shard_map(
        shards,
        mesh=mesh,
        in_specs=(
            split_tokens,
            P("shard", None),
            P(),
            P(),
            split_rows,
            P(None, "tp"),
            split_rows,
            P(),
            P(),
            P(),
            split_rows,
            P(None, "tp"),
            split_rows,
            P(),
            split_tokens,
        ),
        out_specs=(
            split_tokens,
            split_tokens,
            P(),
            P(),
            split_rows,
            P(None, "tp"),
            split_rows,
            P(),
            P(),
            P(),
            split_rows,
            P(None, "tp"),
            split_rows,
            P(),
        ),
        check_vma=False,
    )
```

profile of v0, /device:TPU:0, one launch (start us, length us, event | category | flops | bytes accessed | tf_op | source)
XLA Modules:
  0.0 452.5 jit_solution(4630089942715056786)
XLA Ops:
  0.6 127.7 %forward_layer.2 = (f32[160,1024]{1,0:T(8,128)}, bf16[640,1024]{1,0:T(8,128)(2,1)}, bf16[4,192,640]{2,1,0:T(8,128)(2,1)}, f32[64,2560]{1,0:T(8,128)}, f32[8,2560...) custom-call(bf16[640,1024]{1,0:T(8,128)(2,1)} %bitcast.3, ...), custom_call_target="tpu_custom_call" | custom-call | flops 10737418240 | bytes 16777216 | tf_op jit(solution)/shard_map/forward_layer/pallas_call | solution.py:372
  128.4 95.9 %forward_layer.3 = (f32[160,1024]{1,0:T(8,128)}, bf16[640,1024]{1,0:T(8,128)(2,1)}, bf16[4,192,640]{2,1,0:T(8,128)(2,1)}, f32[64,2560]{1,0:T(8,128)}, f32[8,2560...) custom-call(bf16[640,1024]{1,0:T(8,128)(2,1)} %get-tuple-element.73., ...), custom_call_target="tpu_custom_call" | custom-call | flops 10737418240 | bytes 16777216 | tf_op jit(solution)/shard_map/forward_layer/pallas_call | solution.py:372
  224.3 100.6 %back_layer.2 = (f32[160,1024]{1,0:T(8,128)}, bf16[640,1024]{1,0:T(8,128)(2,1)}, f32[128,256]{1,0:T(8,128)}, f32[128,1024]{1,0:T(8,128)}, f32[128,1024]{1,0:T(8,...) custom-call(bf16[640,1024]{1,0:T(8,128)(2,1)} %bitcast.2, s32[1,4]{1,0:T(1,128)} %refs_2_.7, ...), custom_call_target="tpu_custom_call" | custom-call | flops 28856811520 | bytes 16777216 | tf_op jit(solution)/shard_map/back_layer/pallas_call | solution.py:372
  324.9 120.8 %back_layer.3 = (f32[160,1024]{1,0:T(8,128)}, bf16[640,1024]{1,0:T(8,128)(2,1)}, f32[128,768]{1,0:T(8,128)}, f32[128,256]{1,0:T(8,128)}, f32[128,1024]{1,0:T(8,1...) custom-call(bf16[640,1024]{1,0:T(8,128)(2,1)} %get-tuple-element.89.refs_0_, ...), custom_call_target="tpu_custom_call" | custom-call | flops 28856811520 | bytes 16777216 | tf_op jit(solution)/shard_map/back_layer/pallas_call | solution.py:372
  445.7 6.5 %gather_outputs.1 = (f32[2,128,768]{2,1,0:T(8,128)}, f32[2,128,256]{2,1,0:T(8,128)}, f32[2,128,1024]{2,1,0:T(8,128)}, f32[2,128,1024]{2,1,0:T(8,128)}, bf16[1,64...) custom-call(f32[128,768]{1,0:T(8,128)} %get-tuple-element.107.refs_0, ...), custom_call_target="tpu_custom_call" | custom-call | tf_op jit(solution)/shard_map/gather_outputs/pallas_call | solution.py:1399
where the time goes:
time: 457 us; the launch traced here: 452 us
  Pallas kernels  451 us (99%)
    pallas_call x4, Pallas kernels, run(): pl.pallas_call(body, in_specs=[pl.BlockSpec(memory_space=space) for _, sp...  445 us

commit v1 on v0

--- a/solution.py
+++ b/solution.py
@@ -1127,10 +1127,7 @@
     if plan.final:
         far[13] = far[13].at[two.rows(two.own)]
     load = {index: mover.stay(far[index], near[index]) for index in (0, 1, 2)}
-    if late:
-        mover.near(mover.stay(late_far, late_mid))
-        late.send_first()
-        late.send_second()
+    late_load = mover.stay(late_far, late_mid) if late else None
     if plan.last:
         chunk = rows // 5 if rows % 80 == 0 else rows
 
@@ -1219,6 +1216,10 @@
         if late:
             late.send_third()
 
+    if late:
+        mover.near(late_load)
+        late.send_first()
+        late.send_second()
     mover.near(load[0], load[1], load[2])
     for index in range(3, len(far)):
         load[index] = mover.stay(far[index], near[index])
@@ -1288,6 +1289,8 @@
         return low
 
     def meanwhile():
+        if not plan.final:
+            reduce("qkv")
         own("qkv")
         second_step("up")
         first_step("out")
@@ -1295,12 +1298,11 @@
         early_step()
 
     def halfway():
-        if plan.inside:
-            reduces["qkv"].fold_blocks(3)
-            if plan.final:
-                reduces["qkv"].send_first()
-
-    reduce("qkv")
+        if plan.final:
+            first_step("qkv")
+
+    if plan.final:
+        reduce("qkv")
     two.eager(qkv_part, to_following, meanwhile, halfway)
     if plan.joined:
         late_held[0, 0:8, :] = jnp.zeros((8, late_held.shape[2]), FULL)
@@ -1308,23 +1310,22 @@
         late_held[0, 8:16, :] = local[...]
         final.step()
         final.step()
+    second_step("out")
+    if plan.final:
+        second_step("qkv")
+    rest("out")
     two.have_mate_own()
     two.have_other()
     if plan.joined:
         final.step()
         early_step()
-    second_step("out")
-    rest("out")
+    if plan.final:
+        rest("qkv")
     if plan.joined:
         final.step()
-    if plan.inside:
-        last = reduces["qkv"]
-        if plan.final:
-            second_step("qkv")
-            rest("qkv")
-        else:
-            last.fold_blocks(2, 1, 0)
-            mover.stay(last.mid, mid_out)
+    if plan.inside and not plan.final:
+        reduces["qkv"].fold_blocks(3, 2, 1, 0)
+        mover.stay(reduces["qkv"].mid, mid_out)
     two.have_mate_other()
     if plan.joined:
         final.step()
@@ -1372,7 +1373,9 @@
     for i, (source, stage, _) in enumerate(pairs):
         coming.append(pltpu.make_async_copy(source, stage, into.at[i]))
         coming[-1].start()
-    outs[5][0] = token_grads[...].astype(FULL)
+    work[5][...] = token_grads[...].astype(FULL)
+    going.append(pltpu.make_async_copy(work[5], outs[5].at[0], out_of.at[len(pairs)]))
+    going[-1].start()
     for row, out in enumerate(outs[6:12]):
         out[...] = totals[row * layers : (row + 1) * layers, 0 : out.shape[1]]
     for row, out in enumerate(outs[12:14]):
@@ -1400,12 +1403,12 @@
         functools.partial(gather_outputs_kernel, layers),
         grid=(1,),
         in_specs=[hbm] * len(parts) + [whole(token_grads.shape), hbm, whole(totals.shape)],
-        out_specs=[hbm] * 5 + [whole(shape) for shape in shapes[5:] + small],
+        out_specs=[hbm] * 6 + [whole(shape) for shape in small],
         out_shape=[jax.ShapeDtypeStruct(*pair) for pair in zip(shapes, types)]
         + [jax.ShapeDtypeStruct(shape, FULL) for shape in small],
         scratch_shapes=[VMEM(shape, FULL) for shape in shapes[:4]]
-        + [VMEM((rows, width), LOW)]
-        + [pltpu.SemaphoreType.DMA((copies,)), pltpu.SemaphoreType.DMA((copies,))],
+        + [VMEM((rows, width), LOW), VMEM((rows, width), FULL)]
+        + [pltpu.SemaphoreType.DMA((copies,)), pltpu.SemaphoreType.DMA((copies + 1,))],
         compiler_params=pltpu.CompilerParams(vmem_limit_bytes=60 * 2**20),
         name="gather_outputs",
     )(*parts, token_grads, mixed, totals)

time: 457 us -> 462 us (1.011)
  Pallas kernels: 451 us -> 456 us
where the time goes in v1:
time: 462 us; the launch traced here: 457 us
  Pallas kernels  456 us (99%)
    pallas_call x4, Pallas kernels, run(): pl.pallas_call(body, in_specs=[pl.BlockSpec(memory_space=space) for _, sp...  449 us

profile of v1, /device:TPU:0, one launch (start us, length us, event | category | flops | bytes accessed | tf_op | source)
XLA Modules:
  0.0 457.3 jit_solution(4608325283122897223)
XLA Ops:
  0.6 127.7 %forward_layer.2 = (f32[160,1024]{1,0:T(8,128)}, bf16[640,1024]{1,0:T(8,128)(2,1)}, bf16[4,192,640]{2,1,0:T(8,128)(2,1)}, f32[64,2560]{1,0:T(8,128)}, f32[8,2560...) custom-call(bf16[640,1024]{1,0:T(8,128)(2,1)} %bitcast.3, ...), custom_call_target="tpu_custom_call" | custom-call | flops 10737418240 | bytes 16777216 | tf_op jit(solution)/shard_map/forward_layer/pallas_call | solution.py:372
  128.4 95.9 %forward_layer.3 = (f32[160,1024]{1,0:T(8,128)}, bf16[640,1024]{1,0:T(8,128)(2,1)}, bf16[4,192,640]{2,1,0:T(8,128)(2,1)}, f32[64,2560]{1,0:T(8,128)}, f32[8,2560...) custom-call(bf16[640,1024]{1,0:T(8,128)(2,1)} %get-tuple-element.73., ...), custom_call_target="tpu_custom_call" | custom-call | flops 10737418240 | bytes 16777216 | tf_op jit(solution)/shard_map/forward_layer/pallas_call | solution.py:372
  224.3 100.6 %back_layer.2 = (f32[160,1024]{1,0:T(8,128)}, bf16[640,1024]{1,0:T(8,128)(2,1)}, f32[128,256]{1,0:T(8,128)}, f32[128,1024]{1,0:T(8,128)}, f32[128,1024]{1,0:T(8,...) custom-call(bf16[640,1024]{1,0:T(8,128)(2,1)} %bitcast.2, s32[1,4]{1,0:T(1,128)} %refs_2_.7, ...), custom_call_target="tpu_custom_call" | custom-call | flops 28856811520 | bytes 16777216 | tf_op jit(solution)/shard_map/back_layer/pallas_call | solution.py:372
  324.9 124.9 %back_layer.3 = (f32[160,1024]{1,0:T(8,128)}, bf16[640,1024]{1,0:T(8,128)(2,1)}, f32[128,768]{1,0:T(8,128)}, f32[128,256]{1,0:T(8,128)}, f32[128,1024]{1,0:T(8,1...) custom-call(bf16[640,1024]{1,0:T(8,128)(2,1)} %get-tuple-element.89.refs_0_, ...), custom_call_target="tpu_custom_call" | custom-call | flops 28856811520 | bytes 16777216 | tf_op jit(solution)/shard_map/back_layer/pallas_call | solution.py:372
  449.8 7.2 %gather_outputs.1 = (f32[2,128,768]{2,1,0:T(8,128)}, f32[2,128,256]{2,1,0:T(8,128)}, f32[2,128,1024]{2,1,0:T(8,128)}, f32[2,128,1024]{2,1,0:T(8,128)}, bf16[1,64...) custom-call(f32[128,768]{1,0:T(8,128)} %get-tuple-element.107.refs_0, ...), custom_call_target="tpu_custom_call" | custom-call | tf_op jit(solution)/shard_map/gather_outputs/pallas_call | solution.py:1402

commit v2 on v1

--- a/solution.py
+++ b/solution.py
@@ -1249,7 +1249,6 @@
         if turn == 3:
             second_step("down")
             first_step("up")
-            rest("down")
 
     attend_back_part(
         size,
@@ -1264,7 +1263,7 @@
         attend_work,
         ready,
         waiting,
-        lambda: None,
+        lambda: rest("down"),
         between,
     )
     early_step()
@@ -1294,7 +1293,6 @@
         own("qkv")
         second_step("up")
         first_step("out")
-        rest("up")
         early_step()
 
     def halfway():
@@ -1310,19 +1308,18 @@
         late_held[0, 8:16, :] = local[...]
         final.step()
         final.step()
-    second_step("out")
-    if plan.final:
-        second_step("qkv")
-    rest("out")
     two.have_mate_own()
     two.have_other()
     if plan.joined:
         final.step()
         early_step()
+    second_step("out")
     if plan.final:
-        rest("qkv")
+        second_step("qkv")
     if plan.joined:
         final.step()
+    for name in ("up", "out") + (("qkv",) if plan.final else ()):
+        rest(name)
     if plan.inside and not plan.final:
         reduces["qkv"].fold_blocks(3, 2, 1, 0)
         mover.stay(reduces["qkv"].mid, mid_out)
@@ -1373,9 +1370,7 @@
     for i, (source, stage, _) in enumerate(pairs):
         coming.append(pltpu.make_async_copy(source, stage, into.at[i]))
         coming[-1].start()
-    work[5][...] = token_grads[...].astype(FULL)
-    going.append(pltpu.make_async_copy(work[5], outs[5].at[0], out_of.at[len(pairs)]))
-    going[-1].start()
+    outs[5][0] = token_grads[...].astype(FULL)
     for row, out in enumerate(outs[6:12]):
         out[...] = totals[row * layers : (row + 1) * layers, 0 : out.shape[1]]
     for row, out in enumerate(outs[12:14]):
@@ -1403,12 +1398,12 @@
         functools.partial(gather_outputs_kernel, layers),
         grid=(1,),
         in_specs=[hbm] * len(parts) + [whole(token_grads.shape), hbm, whole(totals.shape)],
-        out_specs=[hbm] * 6 + [whole(shape) for shape in small],
+        out_specs=[hbm] * 5 + [whole(shape) for shape in shapes[5:] + small],
         out_shape=[jax.ShapeDtypeStruct(*pair) for pair in zip(shapes, types)]
         + [jax.ShapeDtypeStruct(shape, FULL) for shape in small],
         scratch_shapes=[VMEM(shape, FULL) for shape in shapes[:4]]
-        + [VMEM((rows, width), LOW), VMEM((rows, width), FULL)]
-        + [pltpu.SemaphoreType.DMA((copies,)), pltpu.SemaphoreType.DMA((copies + 1,))],
+        + [VMEM((rows, width), LOW)]
+        + [pltpu.SemaphoreType.DMA((copies,)), pltpu.SemaphoreType.DMA((copies,))],
         compiler_params=pltpu.CompilerParams(vmem_limit_bytes=60 * 2**20),
         name="gather_outputs",
     )(*parts, token_grads, mixed, totals)

time: 462 us -> 465 us (level)
    pallas_call x4, Pallas kernels: 449 us -> 454 us  [run(): pl.pallas_call(body, in_specs=[pl.BlockSpec(memory_space=space) for _, sp...]
where the time goes in v2:
time: 465 us; the launch traced here: 461 us
  Pallas kernels  460 us (99%)
    pallas_call x4, Pallas kernels, run(): pl.pallas_call(body, in_specs=[pl.BlockSpec(memory_space=space) for _, sp...  454 us

profile of v2, /device:TPU:0, one launch (start us, length us, event | category | flops | bytes accessed | tf_op | source)
XLA Modules:
  0.0 461.4 jit_solution(1472436695538450340)
XLA Ops:
  0.6 127.7 %forward_layer.2 = (f32[160,1024]{1,0:T(8,128)}, bf16[640,1024]{1,0:T(8,128)(2,1)}, bf16[4,192,640]{2,1,0:T(8,128)(2,1)}, f32[64,2560]{1,0:T(8,128)}, f32[8,2560...) custom-call(bf16[640,1024]{1,0:T(8,128)(2,1)} %bitcast.3, ...), custom_call_target="tpu_custom_call" | custom-call | flops 10737418240 | bytes 16777216 | tf_op jit(solution)/shard_map/forward_layer/pallas_call | solution.py:372
  128.4 95.9 %forward_layer.3 = (f32[160,1024]{1,0:T(8,128)}, bf16[640,1024]{1,0:T(8,128)(2,1)}, bf16[4,192,640]{2,1,0:T(8,128)(2,1)}, f32[64,2560]{1,0:T(8,128)}, f32[8,2560...) custom-call(bf16[640,1024]{1,0:T(8,128)(2,1)} %get-tuple-element.73., ...), custom_call_target="tpu_custom_call" | custom-call | flops 10737418240 | bytes 16777216 | tf_op jit(solution)/shard_map/forward_layer/pallas_call | solution.py:372
  224.3 104.9 %back_layer.2 = (f32[160,1024]{1,0:T(8,128)}, bf16[640,1024]{1,0:T(8,128)(2,1)}, f32[128,256]{1,0:T(8,128)}, f32[128,1024]{1,0:T(8,128)}, f32[128,1024]{1,0:T(8,...) custom-call(bf16[640,1024]{1,0:T(8,128)(2,1)} %bitcast.2, s32[1,4]{1,0:T(1,128)} %refs_2_.7, ...), custom_call_target="tpu_custom_call" | custom-call | flops 28856811520 | bytes 16777216 | tf_op jit(solution)/shard_map/back_layer/pallas_call | solution.py:372
  329.2 125.4 %back_layer.3 = (f32[160,1024]{1,0:T(8,128)}, bf16[640,1024]{1,0:T(8,128)(2,1)}, f32[128,768]{1,0:T(8,128)}, f32[128,256]{1,0:T(8,128)}, f32[128,1024]{1,0:T(8,1...) custom-call(bf16[640,1024]{1,0:T(8,128)(2,1)} %get-tuple-element.89.refs_0_, ...), custom_call_target="tpu_custom_call" | custom-call | flops 28856811520 | bytes 16777216 | tf_op jit(solution)/shard_map/back_layer/pallas_call | solution.py:372
  454.6 6.5 %gather_outputs.1 = (f32[2,128,768]{2,1,0:T(8,128)}, f32[2,128,256]{2,1,0:T(8,128)}, f32[2,128,1024]{2,1,0:T(8,128)}, f32[2,128,1024]{2,1,0:T(8,128)}, bf16[1,64...) custom-call(f32[128,768]{1,0:T(8,128)} %get-tuple-element.107.refs_0, ...), custom_call_target="tpu_custom_call" | custom-call | tf_op jit(solution)/shard_map/gather_outputs/pallas_call | solution.py:1397

commit v3 on v2

--- a/solution.py
+++ b/solution.py
@@ -997,8 +997,9 @@
 
 
 class SmallSums:
-    def __init__(self, mover, rows, held, got):
+    def __init__(self, mover, rows, held, got, shared=None):
         self.mover, self.rows, self.held, self.got = mover, rows, held, got
+        self.shared = shared or rows
         self.stage = 0
         mate, far = tp_peers()
         self.peers = [
@@ -1018,7 +1019,11 @@
             mover.take(self.copy)
             at = self.part(stage - 1)
             self.held[stage] = self.held[stage - 1]
-            self.held[stage, at, :] = self.held[stage - 1, at, :] + self.got[stage - 1, at, :]
+            more = self.got[stage - 1, at, :]
+            if stage < 3 and self.shared < self.rows:
+                row = lax.broadcasted_iota(jnp.int32, more.shape, 0)
+                more = jnp.where(row < self.shared, more, 0.0)
+            self.held[stage, at, :] = self.held[stage - 1, at, :] + more
         if stage < len(self.peers):
             at = self.part(stage)
             self.copy = mover.go(
@@ -1117,7 +1122,7 @@
         early_held, early_got, late_held, late_got = [next(work) for _ in range(4)]
         tops = 8 * (plan.others + 1)
         early = SmallSums(mover, tops, early_held, early_got)
-        final = SmallSums(mover, 8, late_held, late_got)
+        final = SmallSums(mover, 8, late_held, late_got, 2)
         everything = [(split, local)] + others
 
     greet(mover, plan.inside)
@@ -1249,6 +1254,7 @@
         if turn == 3:
             second_step("down")
             first_step("up")
+            rest("down")
 
     attend_back_part(
         size,
@@ -1263,7 +1269,7 @@
         attend_work,
         ready,
         waiting,
-        lambda: rest("down"),
+        lambda: None,
         between,
     )
     early_step()
@@ -1293,6 +1299,7 @@
         own("qkv")
         second_step("up")
         first_step("out")
+        rest("up")
         early_step()
 
     def halfway():
@@ -1305,7 +1312,7 @@
     if plan.joined:
         late_held[0, 0:8, :] = jnp.zeros((8, late_held.shape[2]), FULL)
         late_held[0, 0:2, :] = split[0:2, :]
-        late_held[0, 8:16, :] = local[...]
+        late_held[0, 2:3, :] = local[1:2, :]
         final.step()
         final.step()
     two.have_mate_own()
@@ -1314,15 +1321,17 @@
         final.step()
         early_step()
     second_step("out")
-    if plan.final:
-        second_step("qkv")
+    rest("out")
     if plan.joined:
         final.step()
-    for name in ("up", "out") + (("qkv",) if plan.final else ()):
-        rest(name)
-    if plan.inside and not plan.final:
-        reduces["qkv"].fold_blocks(3, 2, 1, 0)
-        mover.stay(reduces["qkv"].mid, mid_out)
+    if plan.inside:
+        last = reduces["qkv"]
+        if plan.final:
+            second_step("qkv")
+            rest("qkv")
+        else:
+            last.fold_blocks(3, 2, 1, 0)
+            mover.stay(last.mid, mid_out)
     two.have_mate_other()
     if plan.joined:
         final.step()
@@ -1342,7 +1351,7 @@
             at = row * len(everything)
             totals[at : at + 1, :] = last_value[row : row + 1, :]
         at = tops + len(everything)
-        totals[at : at + 1, :] = last_value[9:10, :]
+        totals[at : at + 1, :] = last_value[2:3, :]
     if not plan.inside:
         for name, (lhs, rhs) in {
             "down": (grad, hidden),
@@ -1476,8 +1485,8 @@
         scratch += [
             VMEM((6, depth + 8, wide), FULL),
             VMEM((5, depth + 8, wide), FULL),
-            VMEM((6, 16, wide), FULL),
-            VMEM((5, 16, wide), FULL),
+            VMEM((6, 8, wide), FULL),
+            VMEM((5, 8, wide), FULL),
         ]
     results = run(
         functools.partial(back_kernel, plan, size, tile),

time: 465 us -> 455 us (0.978)
  Pallas kernels: 460 us -> 449 us
    pallas_call x4, Pallas kernels: 454 us -> 443 us  [run(): pl.pallas_call(body, in_specs=[pl.BlockSpec(memory_space=space) for _, sp...]
where the time goes in v3:
time: 455 us; the launch traced here: 450 us
  Pallas kernels  449 us (99%)
    pallas_call x4, Pallas kernels, run(): pl.pallas_call(body, in_specs=[pl.BlockSpec(memory_space=space) for _, sp...  443 us

profile of v3, /device:TPU:0, one launch (start us, length us, event | category | flops | bytes accessed | tf_op | source)
XLA Modules:
  0.0 450.4 jit_solution(6309612534055377032)
XLA Ops:
  0.6 127.7 %forward_layer.2 = (f32[160,1024]{1,0:T(8,128)}, bf16[640,1024]{1,0:T(8,128)(2,1)}, bf16[4,192,640]{2,1,0:T(8,128)(2,1)}, f32[64,2560]{1,0:T(8,128)}, f32[8,2560...) custom-call(bf16[640,1024]{1,0:T(8,128)(2,1)} %bitcast.3, ...), custom_call_target="tpu_custom_call" | custom-call | flops 10737418240 | bytes 16777216 | tf_op jit(solution)/shard_map/forward_layer/pallas_call | solution.py:372
  128.4 95.9 %forward_layer.3 = (f32[160,1024]{1,0:T(8,128)}, bf16[640,1024]{1,0:T(8,128)(2,1)}, bf16[4,192,640]{2,1,0:T(8,128)(2,1)}, f32[64,2560]{1,0:T(8,128)}, f32[8,2560...) custom-call(bf16[640,1024]{1,0:T(8,128)(2,1)} %get-tuple-element.73., ...), custom_call_target="tpu_custom_call" | custom-call | flops 10737418240 | bytes 16777216 | tf_op jit(solution)/shard_map/forward_layer/pallas_call | solution.py:372
  224.3 100.6 %back_layer.2 = (f32[160,1024]{1,0:T(8,128)}, bf16[640,1024]{1,0:T(8,128)(2,1)}, f32[128,256]{1,0:T(8,128)}, f32[128,1024]{1,0:T(8,128)}, f32[128,1024]{1,0:T(8,...) custom-call(bf16[640,1024]{1,0:T(8,128)(2,1)} %bitcast.2, s32[1,4]{1,0:T(1,128)} %refs_2_.7, ...), custom_call_target="tpu_custom_call" | custom-call | flops 28856811520 | bytes 16777216 | tf_op jit(solution)/shard_map/back_layer/pallas_call | solution.py:372
  324.9 118.7 %back_layer.3 = (f32[160,1024]{1,0:T(8,128)}, bf16[640,1024]{1,0:T(8,128)(2,1)}, f32[128,768]{1,0:T(8,128)}, f32[128,256]{1,0:T(8,128)}, f32[128,1024]{1,0:T(8,1...) custom-call(bf16[640,1024]{1,0:T(8,128)(2,1)} %get-tuple-element.89.refs_0_, ...), custom_call_target="tpu_custom_call" | custom-call | flops 28856811520 | bytes 16777216 | tf_op jit(solution)/shard_map/back_layer/pallas_call | solution.py:372
  443.6 6.5 %gather_outputs.1 = (f32[2,128,768]{2,1,0:T(8,128)}, f32[2,128,256]{2,1,0:T(8,128)}, f32[2,128,1024]{2,1,0:T(8,128)}, f32[2,128,1024]{2,1,0:T(8,128)}, bf16[1,64...) custom-call(f32[128,768]{1,0:T(8,128)} %get-tuple-element.107.refs_0, ...), custom_call_target="tpu_custom_call" | custom-call | tf_op jit(solution)/shard_map/gather_outputs/pallas_call | solution.py:1406
